TPU v7x, 512 devices: a whole 4x8x8 slice. The times are simulated.
512 devices in a mesh: dp: 16 (over x, z_lo, core), ctx: 32 (over z_hi, y).
Axes of the slice: x: 4, y: 8, z: 8 (z_hi: 4, z_lo: 2; z = z_hi * 2 + z_lo), core: 2. Of those that a mesh axis runs over, the one named last changes fastest.
Arguments:
- queries: bfloat16 [16, 4096, 1024], P('dp', 'ctx'), may hold values from -60 to 60
- keys: bfloat16 [16, 4096, 128], P('dp', 'ctx'), may hold values from -6 to 6
- values: bfloat16 [16, 4096, 192], P('dp', 'ctx'), may hold values from -96 to 96
- features_fine: bfloat16 [16, 8192, 1536], P('dp', 'ctx'), may hold values from -6 to 6
- rc_state: bfloat16 [16, 4096, 1536], P('dp', 'ctx'), may hold values from -6 to 6
- conv_weight: float32 [5, 1536], replicated, may hold values from -2.5 to 2.5
Outputs:
- d_fine: bfloat16 [16, 8192, 1536], P('dp', 'ctx')
- d_weight: float32 [5, 1536], replicated
All inputs are finite; a program needn't handle non-finite values.
Results may differ from a plain program's by a relative error of at most 0.0085.
Values may be sent and summed in bfloat16 or wider, within the bound.
A program may use at most 64 MiB of HBM per device.

v0:
```python
import math
import jax
import jax.numpy as jnp
from jax import lax
from jax.sharding import PartitionSpec as P

HEADS = 8
KW = 5


def padded_2(cells, sides, width):
    for axis, dim in sides:
        count = lax.axis_size(axis)
        ends = count - 1
        head = lax.slice_in_dim(cells, 0, width, axis=dim)
        tail = lax.slice_in_dim(cells, cells.shape[dim] - width, cells.shape[dim], axis=dim)
        cells = jnp.concatenate(
            [
                lax.ppermute(tail, axis, [(i, (i + 1) % count) for i in range(ends)]),
                cells,
                lax.ppermute(head, axis, [((i + 1) % count, i) for i in range(ends)]),
            ],
            axis=dim,
        )
    return cells


def body(queries, keys, values, features_fine, rc_state, conv_weight):
    tok_rows = queries.shape[1]
    key_size = keys.shape[2]
    value_size = values.shape[2]
    q_heads = queries[0].reshape(tok_rows, HEADS, key_size)
    ctx_count = lax.axis_size("ctx")
    run_top = jnp.full((tok_rows, HEADS), -1e30, jnp.float32)
    key_piece = lax.all_gather(keys, "ctx", axis=1, tiled=True)
    value_piece = lax.all_gather(values, "ctx", axis=1, tiled=True)
    scores = jnp.einsum(
        "qhd,kd->qhk", q_heads, key_piece[0], preferred_element_type=jnp.float32
    ) * key_size ** (-0.5)
    new_top = jnp.maximum(run_top, jnp.max(scores, axis=-1))
    expd = jnp.exp(scores - new_top[..., None])
    new_total = jnp.sum(expd, axis=-1)
    mixed = jnp.einsum(
        "qhk,kv->qhv", expd.astype(jnp.bfloat16), value_piece[0], preferred_element_type=jnp.float32
    )
    attended = (mixed / new_total[..., None]).reshape(tok_rows, HEADS * value_size)[None]
    padded = padded_2(features_fine, (("ctx", 1),), 2)
    taps = [padded[:, k : k + 2 * tok_rows : 2, :].astype(jnp.float32) for k in range(KW)]
    coarse = conv_weight[0] * taps[0]
    for k in range(1, KW):
        coarse = coarse + conv_weight[k] * taps[k]
    slices = lax.all_to_all(rc_state, "ctx", split_axis=2, concat_axis=0, tiled=True)
    flipped = slices[::-1]
    mirrored = lax.all_to_all(flipped, "ctx", split_axis=0, concat_axis=2, tiled=True)
    grad = coarse + attended - mirrored[:, ::-1, :].astype(jnp.float32)
    gpad = padded_2(grad.astype(jnp.bfloat16), (("ctx", 1),), 1).astype(grad.dtype)
    even = (
        conv_weight[0] * gpad[:, 2:]
        + conv_weight[2] * gpad[:, 1:-1]
        + conv_weight[4] * gpad[:, :-2]
    )
    odd = conv_weight[1] * gpad[:, 2:] + conv_weight[3] * gpad[:, 1:-1]
    d_fine = (
        jnp.stack([even, odd], axis=2)
        .reshape(grad.shape[0], 2 * tok_rows, grad.shape[2])
        .astype(jnp.bfloat16)
    )
    partial_grad = jnp.stack([jnp.sum(grad * taps[k], axis=(0, 1)) for k in range(KW)])
    summed = lax.psum(partial_grad, ("dp", "ctx"))
    scale = 1.0 / math.sqrt(lax.axis_size("dp") * tok_rows * ctx_count)
    return (d_fine, summed * scale)


def solution(mesh):
    placed = (
        P("dp", "ctx", None),
        P("dp", "ctx", None),
        P("dp", "ctx", None),
        P("dp", "ctx", None),
        P("dp", "ctx", None),
        P(),
    )
    return jax.shard_map(
        body, mesh=mesh, in_specs=placed, out_specs=(P("dp", "ctx", None), P()), check_vma=False
    )
```

profile of v0, /device:TPU:184, one launch (start us, length us, event | category | flops | bytes accessed | tf_op | source)
XLA Modules:
  0.0 341.5 jit_solution(18383458230890813925)
XLA Ops:
  7.2 0.0 all-gather.3.cloned.1.call-start
  7.2 0.7 all-gather.3.cloned.1.call-update
  7.9 2.2 copy.29
  10.1 0.5 broadcast.15
  10.6 8.8 %reduce.10 = bf16[1536,128]{1,0:T(8,128)(2,1)S(1)} reduce(bf16[1536,1,128]{2,1,0:T(2,128)(2,1)S(1)} %bitcast.34, bf16[]{:T(256)} %broadcast.15), dimensions={1}, to_apply=%bitcast.29.reduce_sub_computation | reduce | bytes 786434
  19.4 0.8 reshape.84
  20.2 13.8 %all-to-all-start = ((bf16[32,2,3072]{2,1,0:T(2,128)(2,1)}), bf16[32,2,3072]{2,1,0:T(2,128)(2,1)S(1)}, u32[]{:S(2)}, u32[]{:S(2)}) async-start(bf16[32,2,3072]{2,1,0:T(2,128)(2,1)} %reshape.84), calls=%async_computation | async-start | bytes 786432 | tf_op jit(solution)/shard_map/all_to_all | solution.py:52
  34.0 0.0 all-gather.5.cloned.1.call-start
  34.1 0.7 all-gather.5.cloned.1.call-update
  34.8 12.8 %all-to-all-done = bf16[32,2,3072]{2,1,0:T(2,128)(2,1)S(1)} async-done(((bf16[32,2,3072]{2,1,0:T(2,128)(2,1)}), bf16[32,2,3072]{2,1,0:T(2,128)(2,1)S(1)}, u32[]{:S(2)}, u32[]{:S(2)}) %all-to-all-start) | async-done | bytes 393248 | tf_op jit(solution)/shard_map/all_to_all | solution.py:52
  47.6 0.3 reshape.85
  47.9 0.1 copy.31
  48.0 0.8 rev.6
  48.7 8.5 %all-to-all-start.1 = ((bf16[32,128,48]{1,2,0:T(8,128)(2,1)}), bf16[32,128,48]{1,2,0:T(8,128)(2,1)S(1)}, u32[]{:S(2)}, u32[]{:S(2)}) async-start(bf16[32,128,48]{1,2,0:T(8,128)(2,1)} %rev.6), calls=%async_computation.1 | async-start | bytes 786432 | tf_op jit(solution)/shard_map/all_to_all | solution.py:54
  57.3 0.3 copy.24
  57.5 5.5 %collective-permute-start = (bf16[1,2,1536]{1,2,0:T(8,128)(2,1)S(1)}, bf16[1,2,1536]{1,2,0:T(8,128)(2,1)}, u32[]{:S(2)}, u32[]{:S(2)}) collective-permute-start(bf16[1,2,1536]{1,2,0:T(8,128)(2,1)S(1)} %copy.24), channel_id=1, source_target_pairs={{0,1},{1,2},{2,3},{3,4},{4,5},{5,6},{6,7},{7,8},{8,9},{9,10},{10,1... | collective-permute-start | bytes 18440 | tf_op jit(solution)/shard_map/ppermute | solution.py:19
  63.0 0.3 copy.25
  63.3 2.1 collective-permute-start.1
  65.4 0.1 slice_reduce_fusion.4
  65.5 0.3 copy.26
  65.8 1.0 copy.32
  66.8 14.4 %slice.65 = bf16[1,128,1536]{1,2,0:T(8,128)(2,1)S(1)} slice(bf16[1,256,1536]{1,2,0:T(8,128)(2,1)S(1)} %copy.26), slice={[0:1:1], [0:256:2], [0:1536:1]} | slice | bytes 786432 | tf_op jit(solution)/shard_map/slice | solution.py:48
  81.2 5.9 %collective-permute-done.1 = bf16[1,2,1536]{1,2,0:T(8,128)(2,1)} collective-permute-done((bf16[1,2,1536]{1,2,0:T(8,128)(2,1)S(1)}, bf16[1,2,1536]{1,2,0:T(8,128)(2,1)}, u32[]{:S(2)}, u32[]{:S(2)}) %collective-permute-start.1) | collective-permute-done | bytes 6176 | tf_op jit(solution)/shard_map/ppermute | solution.py:21
  87.1 1.8 pad_maximum_fusion
  88.9 14.4 %slice.61 = bf16[1,128,1536]{1,2,0:T(8,128)(2,1)S(1)} slice(bf16[1,260,1536]{1,2,0:T(8,128)(2,1)S(1)} %pad_maximum_fusion), slice={[0:1:1], [0:256:2], [0:1536:1]} | slice | bytes 786432 | tf_op jit(solution)/shard_map/slice | solution.py:48
  103.3 14.4 %slice.63 = bf16[1,128,1536]{1,2,0:T(8,128)(2,1)S(1)} slice(bf16[1,260,1536]{1,2,0:T(8,128)(2,1)S(1)} %pad_maximum_fusion), slice={[0:1:1], [1:257:2], [0:1536:1]} | slice | bytes 786432 | tf_op jit(solution)/shard_map/slice | solution.py:48
  117.7 14.7 %slice.67 = bf16[1,128,1536]{1,2,0:T(8,128)(2,1)S(1)} slice(bf16[1,260,1536]{1,2,0:T(8,128)(2,1)S(1)} %pad_maximum_fusion), slice={[0:1:1], [3:259:2], [0:1536:1]} | slice | bytes 786432 | tf_op jit(solution)/shard_map/slice | solution.py:48
  132.4 15.0 %slice.69 = bf16[1,128,1536]{1,2,0:T(8,128)(2,1)} slice(bf16[1,260,1536]{1,2,0:T(8,128)(2,1)S(1)} %pad_maximum_fusion), slice={[0:1:1], [4:260:2], [0:1536:1]} | slice | bytes 786432 | tf_op jit(solution)/shard_map/slice | solution.py:48
  147.4 1.3 rev.7
  148.7 0.0 all-gather.3.cloned.1.call-done
  148.8 9.3 %multiply_reduce_fusion = (f32[128,8]{0,1:T(8,128)S(1)}, f32[128,8,4096]{2,0,1:T(8,128)}) fusion(bf16[1,4096,128]{2,1,0:T(8,128)(2,1)} %all-gather.3.cloned.1.call-done, bf16[128,8,128]{2,1,0:T(8,128)(2,1)S(1)} %bitcast.36), kind=kOutput, calls=%fused_computation.1 | convolution fusion | flops 1082129408 | bytes 18092032 | tf_op jit(solution)/shard_map/qhd,kd->qhk/dot_general | solution.py:37
  158.0 8.6 %fusion = f32[128,8]{0,1:T(8,128)S(1)} fusion(f32[128,8,4096]{2,0,1:T(8,128)} %get-tuple-element.20, f32[128,8]{0,1:T(8,128)S(1)} %broadcast_maximum_fusion), kind=kLoop, calls=%fused_computation.2 | loop fusion | flops 12581888 | bytes 16785408 | tf_op jit(solution)/shard_map/reduce_sum | solution.py:42
  166.7 29.0 %all-gather.5.cloned.1.call-done = bf16[1,4096,192]{1,2,0:T(8,128)(2,1)} async-done(((bf16[1,128,192]{1,2,0:T(8,128)(2,1)}), bf16[1,4096,192]{1,2,0:T(8,128)(2,1)}) %all-gather.5.cloned.1.call-update) | async-done | bytes 1572880 | tf_op jit(solution)/shard_map/all_gather | solution.py:36
  195.6 8.0 %fusion.7 = f32[128,8,192]{0,2,1:T(8,128)S(1)} fusion(bf16[1,4096,192]{1,2,0:T(8,128)(2,1)} %all-gather.5.cloned.1.call-done, f32[128,8,4096]{2,0,1:T(8,128)} %get-tuple-element.20, f32[128,8]{0,1:T(8,128)S(1)} %broadcast_maximum_fusion, f32[128,8]{0,1:T(8,128)S(1)} %fusion), kind=kOutput, calls=%fused_computation.19 | convolution fusion | flops 1623392256 | bytes 19144704 | tf_op jit(solution)/shard_map/qhk,kv->qhv/dot_general | solution.py:43
  203.6 2.7 fusion.22
  206.4 0.1 stack.38
  206.5 93.2 %psum.7 = f32[5,1536]{1,0:T(8,128)S(1)} all-reduce(f32[5,1536]{1,0:T(8,128)S(1)} %stack.38), channel_id=1, replica_groups=mesh['dp'=16,'ctx'=32] {'dp','ctx'}, use_global_device_ids=true, to_apply=%region_7.0 | all-reduce | flops 7680 | bytes 61440 | tf_op jit(solution)/shard_map/psum | solution.py:69
  299.7 0.2 fusion.31
  299.9 6.2 %collective-permute-start.2 = (bf16[1,1,1536]{1,2,0:T(8,128)(2,1)S(1)}, bf16[1,1,1536]{1,2,0:T(8,128)(2,1)S(1)}, u32[]{:S(2)}, u32[]{:S(2)}) collective-permute-start(bf16[1,1,1536]{1,2,0:T(8,128)(2,1)S(1)} %get-tuple-element.17), channel_id=1, source_target_pairs={{0,1},{1,2},{2,3},{3,4},{4,5},{5,6},{6,7},{7,8},{8,9},{9,10},{10,1... | collective-permute-start | bytes 9224 | tf_op jit(solution)/shard_map/ppermute | solution.py:19
  306.1 1.9 collective-permute-start.3
  308.0 0.6 broadcast_multiply_fusion
  308.6 11.6 %collective-permute-done.2 = bf16[1,1,1536]{1,2,0:T(8,128)(2,1)S(1)} collective-permute-done((bf16[1,1,1536]{1,2,0:T(8,128)(2,1)S(1)}, bf16[1,1,1536]{1,2,0:T(8,128)(2,1)S(1)}, u32[]{:S(2)}, u32[]{:S(2)}) %collective-permute-start.2) | collective-permute-done | bytes 3104 | tf_op jit(solution)/shard_map/ppermute | solution.py:19
  320.2 10.3 %collective-permute-done.3 = bf16[1,1,1536]{1,2,0:T(8,128)(2,1)S(1)} collective-permute-done((bf16[1,1,1536]{1,2,0:T(8,128)(2,1)S(1)}, bf16[1,1,1536]{1,2,0:T(8,128)(2,1)S(1)}, u32[]{:S(2)}, u32[]{:S(2)}) %collective-permute-start.3) | collective-permute-done | bytes 3104 | tf_op jit(solution)/shard_map/ppermute | solution.py:21
  330.5 0.4 maximum_convert_fusion
  330.9 1.7 fusion.26
  332.6 0.1 pad_maximum_fusion.1
  332.7 0.8 copy.30
  333.5 1.2 convert_element_type.56
  (15 shorter events, 0.1 us)
Async XLA Ops:
  7.2 141.6 %all-gather.3.cloned.1.call-start = ((), (), s32[]{:S(2)}) async-start(), calls=%async_computation.2 | async-start | bytes 1081344 | tf_op jit(solution)/shard_map/all_gather | solution.py:35
  20.2 37.0 %copy-start.1 = (bf16[1,256,1536]{2,1,0:T(8,128)(2,1)S(1)}, bf16[1,256,1536]{2,1,0:T(8,128)(2,1)}, u32[]{:S(2)}) copy-start(bf16[1,256,1536]{2,1,0:T(8,128)(2,1)} %param.9) | copy-start | bytes 2359300
  20.2 27.4 %all-to-all-start = ((bf16[32,2,3072]{2,1,0:T(2,128)(2,1)}), bf16[32,2,3072]{2,1,0:T(2,128)(2,1)S(1)}, u32[]{:S(2)}, u32[]{:S(2)}) async-start(bf16[32,2,3072]{2,1,0:T(2,128)(2,1)} %reshape.84), calls=%async_computation | async-start | bytes 786432 | tf_op jit(solution)/shard_map/all_to_all | solution.py:52
  34.0 161.6 %all-gather.5.cloned.1.call-start = ((), (), s32[]{:S(2)}) async-start(), calls=%async_computation.3 | async-start | bytes 1622016 | tf_op jit(solution)/shard_map/all_gather | solution.py:36
  34.8 30.6 %copy-start.2 = (f32[5,1536]{1,0:T(8,128)S(1)}, f32[5,1536]{1,0:T(8,128)}, u32[]{:S(2)}) copy-start(f32[5,1536]{1,0:T(8,128)} %param.11) | copy-start | bytes 92164
  48.7 98.6 %all-to-all-start.1 = ((bf16[32,128,48]{1,2,0:T(8,128)(2,1)}), bf16[32,128,48]{1,2,0:T(8,128)(2,1)S(1)}, u32[]{:S(2)}, u32[]{:S(2)}) async-start(bf16[32,128,48]{1,2,0:T(8,128)(2,1)} %rev.6), calls=%async_computation.1 | async-start | bytes 786432 | tf_op jit(solution)/shard_map/all_to_all | solution.py:54
  57.5 23.6 %collective-permute-start = (bf16[1,2,1536]{1,2,0:T(8,128)(2,1)S(1)}, bf16[1,2,1536]{1,2,0:T(8,128)(2,1)}, u32[]{:S(2)}, u32[]{:S(2)}) collective-permute-start(bf16[1,2,1536]{1,2,0:T(8,128)(2,1)S(1)} %copy.24), channel_id=1, source_target_pairs={{0,1},{1,2},{2,3},{3,4},{4,5},{5,6},{6,7},{7,8},{8,9},{9,10},{10,1... | collective-permute-start | bytes 18440 | tf_op jit(solution)/shard_map/ppermute | solution.py:19
  63.3 23.8 %collective-permute-start.1 = (bf16[1,2,1536]{1,2,0:T(8,128)(2,1)S(1)}, bf16[1,2,1536]{1,2,0:T(8,128)(2,1)}, u32[]{:S(2)}, u32[]{:S(2)}) collective-permute-start(bf16[1,2,1536]{1,2,0:T(8,128)(2,1)S(1)} %copy.25), channel_id=1, source_target_pairs={{1,0},{2,1},{3,2},{4,3},{5,4},{6,5},{7,6},{8,7},{9,8},{10,9},{11,1... | collective-permute-start | bytes 18440 | tf_op jit(solution)/shard_map/ppermute | solution.py:21
  166.7 36.9 %copy-start = (bf16[1,128,1536]{1,2,0:T(8,128)(2,1)S(1)}, bf16[1,128,1536]{1,2,0:T(8,128)(2,1)}, u32[]{:S(2)}) copy-start(bf16[1,128,1536]{1,2,0:T(8,128)(2,1)} %slice.69) | copy-start | bytes 1179652
  299.9 20.3 %collective-permute-start.2 = (bf16[1,1,1536]{1,2,0:T(8,128)(2,1)S(1)}, bf16[1,1,1536]{1,2,0:T(8,128)(2,1)S(1)}, u32[]{:S(2)}, u32[]{:S(2)}) collective-permute-start(bf16[1,1,1536]{1,2,0:T(8,128)(2,1)S(1)} %get-tuple-element.17), channel_id=1, source_target_pairs={{0,1},{1,2},{2,3},{3,4},{4,5},{5,6},{6,7},{7,8},{8,9},{9,10},{10,1... | collective-permute-start | bytes 9224 | tf_op jit(solution)/shard_map/ppermute | solution.py:19
  306.1 24.4 %collective-permute-start.3 = (bf16[1,1,1536]{1,2,0:T(8,128)(2,1)S(1)}, bf16[1,1,1536]{1,2,0:T(8,128)(2,1)S(1)}, u32[]{:S(2)}, u32[]{:S(2)}) collective-permute-start(bf16[1,1,1536]{1,2,0:T(8,128)(2,1)S(1)} %get-tuple-element.18), channel_id=1, source_target_pairs={{1,0},{2,1},{3,2},{4,3},{5,4},{6,5},{7,6},{8,7},{9,8},{10,9},{11,1... | collective-permute-start | bytes 9224 | tf_op jit(solution)/shard_map/ppermute | solution.py:21
Sparse Core Ops, SparseCore 0:
  11.2 102.2 all-gather.2
  116.5 79.0 all-gather.4
where the time goes:
time: 342 us; the launch traced here: 341 us
  blocking collectives  93.2 us (27%)
  local copies, waits for them, and re-layouts  82.9 us (24%)
  waiting for transfers between devices  70.9 us (21%)
  starting transfers between devices  38.1 us (11%)
  other arithmetic  24.9 us (7%)
  matrix products  17.2 us (5%)
  between operations  14.3 us (4%)
    psum x1, blocking collectives, body(): summed = lax.psum(partial_grad, ('dp', 'ctx'))  93.2 us
    slice x5, local copies, waits for them, and re-layouts, body(): padded[:, k:k + 2 * tok_rows:2, :].astype(jnp.float32)  72.8 us
    all_gather x1, waiting for transfers between devices, body(): value_piece = lax.all_gather(values, 'ctx', axis=1, tiled=True)  29 us
    ppermute x2, waiting for transfers between devices, padded_2(): lax.ppermute(head, axis, [((i + 1) % count, i) for i in range(ends)])  16.2 us
    all_to_all x1, starting transfers between devices, body(): lax.all_to_all(rc_state, 'ctx', split_axis=2, concat_axis=0, tiled=True)  13.8 us
    all_to_all x1, waiting for transfers between devices, body(): lax.all_to_all(rc_state, 'ctx', split_axis=2, concat_axis=0, tiled=True)  12.8 us
    ppermute x2, starting transfers between devices, padded_2(): lax.ppermute(tail, axis, [(i, (i + 1) % count) for i in range(ends)])  11.7 us
    ppermute x2, waiting for transfers between devices, padded_2(): lax.ppermute(tail, axis, [(i, (i + 1) % count) for i in range(ends)])  11.6 us
  transfers between devices with their start and end apart: 8, of which 5 were waited for; matrix products, arithmetic and copies ran while one was open for 32% of the time, Pallas kernels for 0%

commit v1 on v0

--- a/solution.py
+++ b/solution.py
@@ -66,7 +66,8 @@
         .astype(jnp.bfloat16)
     )
     partial_grad = jnp.stack([jnp.sum(grad * taps[k], axis=(0, 1)) for k in range(KW)])
-    summed = lax.psum(partial_grad, ("dp", "ctx"))
+    parts = lax.all_gather(partial_grad, ("dp", "ctx"), axis=0, tiled=False)
+    summed = parts.sum(axis=0)
     scale = 1.0 / math.sqrt(lax.axis_size("dp") * tok_rows * ctx_count)
     return (d_fine, summed * scale)
 

time: 342 us -> 1680 us (4.91)
  the two profiles are of different devices: /device:TPU:184 before, /device:TPU:194 now
where the time goes in v1:
time: 1680 us
  waiting for transfers between devices  1490 us (89%)
  local copies, waits for them, and re-layouts  83.5 us (5%)
  starting transfers between devices  35.5 us (2%)
  other arithmetic  34.8 us (2%)
  matrix products  17.2 us (1%)
    all_gather x1, waiting for transfers between devices, body(): parts = lax.all_gather(partial_grad, ('dp', 'ctx'), axis=0, tiled=False)  1430 us
    slice x5, local copies, waits for them, and re-layouts, body(): padded[:, k:k + 2 * tok_rows:2, :].astype(jnp.float32)  72.8 us
  transfers between devices with their start and end apart: 9, of which 6 were waited for; matrix products, arithmetic and copies ran while one was open for 7% of the time, Pallas kernels for 0%

profile of v1, /device:TPU:194, one launch (start us, length us, event | category | flops | bytes accessed | tf_op | source)
XLA Modules:
  0.0 1679.3 jit_solution(1986093536371174781)
XLA Ops:
  7.2 0.7 all-gather.6.cloned.1.call-update
  7.9 2.2 copy.29
  10.1 0.5 broadcast.15
  10.6 8.8 reduce.11
  19.4 0.8 reshape.88
  20.2 13.7 all-to-all-start
  33.9 0.0 all-gather.8.cloned.1.call-start
  34.0 0.7 all-gather.8.cloned.1.call-update
  34.7 15.1 all-to-all-done
  49.8 0.3 reshape.89
  50.2 0.1 copy.31
  50.2 0.8 rev.6
  51.0 6.1 all-to-all-start.1
  57.1 0.0 all-gather.10.cloned.1.call-start
  57.2 0.3 copy.25
  57.5 4.6 collective-permute-start.1
  62.0 0.3 copy.24
  62.3 2.1 collective-permute-start
  64.4 0.1 slice_reduce_fusion.4
  64.5 0.3 copy.26
  64.8 1.0 copy.32
  65.8 14.4 slice.65
  80.2 0.7 collective-permute-done.1
  80.9 5.6 collective-permute-done
  86.5 1.8 pad_maximum_fusion
  88.4 14.7 slice.69
  103.0 14.7 slice.67
  117.7 14.4 slice.63
  132.1 14.7 slice.61
  146.9 1.3 rev.7
  148.2 9.3 multiply_reduce_fusion
  157.5 8.6 fusion
  166.1 28.7 %all-gather.8.cloned.1.call-done = bf16[1,4096,192]{1,2,0:T(8,128)(2,1)} async-done(((bf16[1,128,192]{1,2,0:T(8,128)(2,1)}), bf16[1,4096,192]{1,2,0:T(8,128)(2,1)}) %all-gather.8.cloned.1.call-update) | async-done | bytes 1572880 | tf_op jit(solution)/shard_map/all_gather | solution.py:36
  194.8 8.0 fusion.7
  202.8 2.7 fusion.22
  205.6 0.7 stack.38
  206.3 0.2 fusion.31
  206.5 2.4 collective-permute-start.2
  208.9 6.5 collective-permute-start.3
  215.3 11.3 collective-permute-done.2
  226.6 0.4 maximum_convert_fusion
  227.0 1.7 fusion.26
  228.7 0.1 pad_maximum_fusion.1
  228.8 0.8 copy.30
  229.6 1.2 convert_element_type.56
  230.8 1431.4 %all-gather.10.cloned.1.call-done = f32[512,5,1536]{2,1,0:T(8,128)} async-done(((f32[1,5,1536]{2,1,0:T(8,128)}), f32[512,5,1536]{2,1,0:T(8,128)}) %all-gather.10.cloned.1.call-update) | async-done | bytes 15728656 | tf_op jit(solution)/shard_map/all_gather | solution.py:69
  1662.2 10.0 reduce_sum.69
  1672.1 0.6 broadcast_multiply_fusion
  (18 shorter events, 0.1 us)
Async XLA Ops:
  7.2 141.0 %all-gather.6.cloned.1.call-start = ((), (), s32[]{:S(2)}) async-start(), calls=%async_computation.2 | async-start | bytes 1081344 | tf_op jit(solution)/shard_map/all_gather | solution.py:35
  20.2 36.9 %copy-start.1 = (bf16[1,256,1536]{2,1,0:T(8,128)(2,1)S(1)}, bf16[1,256,1536]{2,1,0:T(8,128)(2,1)}, u32[]{:S(2)}) copy-start(bf16[1,256,1536]{2,1,0:T(8,128)(2,1)} %param.9) | copy-start | bytes 2359300
  20.2 29.6 %all-to-all-start = ((bf16[32,2,3072]{2,1,0:T(2,128)(2,1)}), bf16[32,2,3072]{2,1,0:T(2,128)(2,1)S(1)}, u32[]{:S(2)}, u32[]{:S(2)}) async-start(bf16[32,2,3072]{2,1,0:T(2,128)(2,1)} %reshape.88), calls=%async_computation | async-start | bytes 786432 | tf_op jit(solution)/shard_map/all_to_all | solution.py:52
  33.9 160.9 %all-gather.8.cloned.1.call-start = ((), (), s32[]{:S(2)}) async-start(), calls=%async_computation.3 | async-start | bytes 1622016 | tf_op jit(solution)/shard_map/all_gather | solution.py:36
  34.7 29.7 %copy-start.2 = (f32[5,1536]{1,0:T(8,128)S(1)}, f32[5,1536]{1,0:T(8,128)}, u32[]{:S(2)}) copy-start(f32[5,1536]{1,0:T(8,128)} %param.11) | copy-start | bytes 92164
  51.0 95.9 %all-to-all-start.1 = ((bf16[32,128,48]{1,2,0:T(8,128)(2,1)}), bf16[32,128,48]{1,2,0:T(8,128)(2,1)S(1)}, u32[]{:S(2)}, u32[]{:S(2)}) async-start(bf16[32,128,48]{1,2,0:T(8,128)(2,1)} %rev.6), calls=%async_computation.1 | async-start | bytes 786432 | tf_op jit(solution)/shard_map/all_to_all | solution.py:54
  57.1 1605.0 %all-gather.10.cloned.1.call-start = ((), (), s32[]{:S(2)}) async-start(), calls=%async_computation.4 | async-start | bytes 25214976 | tf_op jit(solution)/shard_map/all_gather | solution.py:69
  57.5 23.4 %collective-permute-start.1 = (bf16[1,2,1536]{1,2,0:T(8,128)(2,1)S(1)}, bf16[1,2,1536]{1,2,0:T(8,128)(2,1)}, u32[]{:S(2)}, u32[]{:S(2)}) collective-permute-start(bf16[1,2,1536]{1,2,0:T(8,128)(2,1)S(1)} %copy.25), channel_id=1, source_target_pairs={{1,0},{2,1},{3,2},{4,3},{5,4},{6,5},{7,6},{8,7},{9,8},{10,9},{11,1... | collective-permute-start | bytes 18440 | tf_op jit(solution)/shard_map/ppermute | solution.py:21
  62.3 24.2 %collective-permute-start = (bf16[1,2,1536]{1,2,0:T(8,128)(2,1)S(1)}, bf16[1,2,1536]{1,2,0:T(8,128)(2,1)}, u32[]{:S(2)}, u32[]{:S(2)}) collective-permute-start(bf16[1,2,1536]{1,2,0:T(8,128)(2,1)S(1)} %copy.24), channel_id=1, source_target_pairs={{0,1},{1,2},{2,3},{3,4},{4,5},{5,6},{6,7},{7,8},{8,9},{9,10},{10,1... | collective-permute-start | bytes 18440 | tf_op jit(solution)/shard_map/ppermute | solution.py:19
  166.1 36.6 %copy-start = (bf16[1,128,1536]{1,2,0:T(8,128)(2,1)S(1)}, bf16[1,128,1536]{1,2,0:T(8,128)(2,1)}, u32[]{:S(2)}) copy-start(bf16[1,128,1536]{1,2,0:T(8,128)(2,1)} %slice.61) | copy-start | bytes 1179652
  206.5 20.1 %collective-permute-start.2 = (bf16[1,1,1536]{1,2,0:T(8,128)(2,1)S(1)}, bf16[1,1,1536]{1,2,0:T(8,128)(2,1)S(1)}, u32[]{:S(2)}, u32[]{:S(2)}) collective-permute-start(bf16[1,1,1536]{1,2,0:T(8,128)(2,1)S(1)} %get-tuple-element.17), channel_id=1, source_target_pairs={{0,1},{1,2},{2,3},{3,4},{4,5},{5,6},{6,7},{7,8},{8,9},{9,10},{10,1... | collective-permute-start | bytes 9224 | tf_op jit(solution)/shard_map/ppermute | solution.py:19
  208.9 17.7 %collective-permute-start.3 = (bf16[1,1,1536]{1,2,0:T(8,128)(2,1)S(1)}, bf16[1,1,1536]{1,2,0:T(8,128)(2,1)S(1)}, u32[]{:S(2)}, u32[]{:S(2)}) collective-permute-start(bf16[1,1,1536]{1,2,0:T(8,128)(2,1)S(1)} %get-tuple-element.18), channel_id=1, source_target_pairs={{1,0},{2,1},{3,2},{4,3},{5,4},{6,5},{7,6},{8,7},{9,8},{10,9},{11,1... | collective-permute-start | bytes 9224 | tf_op jit(solution)/shard_map/ppermute | solution.py:21
Sparse Core Ops, SparseCore 0:
  11.2 100.9 all-gather.5
  115.3 79.5 all-gather.7
  206.4 1455.6 all-gather.9
